TPU v7x, 32 devices: a whole 2x2x4 slice. The times are simulated.
32 devices in a mesh: brick: 8 (over z, x), scene: 4 (over y, core).
Axes of the slice: x: 2, y: 2, z: 4, core: 2. Of those that a mesh axis runs over, the one named last changes fastest.
Arguments:
- features: float32 [4, 32, 64, 512], P('scene', 'brick'), may hold values from -6 to 6
- cotangent: float32 [4, 32, 64, 512], P('scene', 'brick'), may hold values from -6 to 6
- first_kernel: float32 [27, 64, 64], replicated, may hold values from -0.15625 to 0.15625
- second_kernel: float32 [27, 64, 64], replicated, may hold values from -0.15625 to 0.15625
- counts: int32 [8], P('brick'), may hold values from 1 to 4, as said below
- neighbours: int32 [32, 26], P('brick'), may hold values from -1 to 31, as said below
Outputs:
- out_features: float32 [4, 32, 64, 512], P('scene', 'brick')
- feature_grad: float32 [4, 32, 64, 512], P('scene', 'brick')
- first_grad: float32 [27, 64, 64], replicated
- second_grad: float32 [27, 64, 64], replicated
Inputs may be any that keep to these rules, and one draw needn't show every extreme that they name: Index d of brick owns counts[d] bricks in its slots 0 to counts[d] - 1; some index owns 4. `neighbours`: entries name occupied slots; the relation is symmetric (if slot t is the neighbour of s in direction (a, b, c), s is the neighbour of t in (-a, -b, -c)); unoccupied slots have only -1. A neighbour in a direction with c = 0 is owned by the same index of brick, with c = 1 by the same or the next index, with c = -1 by the same or the previous index.
All inputs are finite; a program needn't handle non-finite values.
Results may differ from a plain program's by a relative error of at most 0.0057.
Values may be sent and summed in bfloat16 or wider, within the bound.
A program may use at most 128 MiB of HBM per device.

v0:
```python
import functools

import jax
import jax.numpy as jnp
from jax import lax
from jax.experimental import pallas as pl
from jax.experimental.pallas import tpu as pltpu
from jax.sharding import PartitionSpec as P

E = 8
G = E + 2
R = 24
L = 128
MESH = pl.DeviceIdType.MESH
F32, BF16 = jnp.float32, jnp.bfloat16

offsets = [(a, b, c) for a in (-1, 0, 1) for b in (-1, 0, 1) for c in (-1, 0, 1)]
directions = [item for item in offsets if item != (0, 0, 0)]
number_of = {item: n for n, item in enumerate(directions)}


def left(shape):
    return lax.broadcasted_iota(jnp.int32, shape, 1) < L // 2


def swap(v):
    return pltpu.roll(v, L // 2, 1)


def sigmoid(v):
    return 1.0 / (1.0 + jnp.exp(-v))


def kernel(
    nb, S,
    f_ref, g_ref, w1_ref, w2_ref, counts_ref, nbr_ref,
    out_ref, fg_ref, g1_ref, g2_ref,
    pad, x1, x2, x3, w1f, w2f, w1b, w2b, et,
    fin, fup, fpre, fhid, fout, low, high, sbuf, rlow, rhigh,
    send_sem, recv_sem,
):
    C = w1_ref.shape[1]
    me = lax.axis_index("brick")
    rows = E * S * E
    jr = S * E

    barrier = pltpu.get_barrier_semaphore()

    @pl.when(me > 0)
    def _():
        pl.semaphore_signal(barrier, inc=1, device_id={"brick": me - 1}, device_id_type=MESH)

    @pl.when(me < nb - 1)
    def _():
        pl.semaphore_signal(barrier, inc=1, device_id={"brick": me + 1}, device_id_type=MESH)

    def at(s, i, j):
        return ((s * G + i) * G + j) * R

    count = counts_ref[0]
    for s in range(S):
        both = jnp.concatenate([f_ref[0, s], g_ref[0, s]], axis=0).T
        both = jnp.where(s < count, both, 0.0)
        other = swap(both)
        m = left(both.shape)
        f = jnp.where(m, both, other)
        g = jnp.where(m, other, both)
        for i in range(E):
            for j in range(E):
                p = (i * E + j) * E
                fin[i, pl.ds(j * jr + s * E, E), :] = f[p : p + E]
                fup[i, pl.ds(j * jr + s * E, E), :] = g[p : p + E]
                pad[pl.ds(at(s, i + 1, j + 1) + E, E), :] = f[p : p + E]

    low[...] = jnp.zeros_like(low)
    high[...] = jnp.zeros_like(high)

    pl.semaphore_wait(barrier, jnp.where(me > 0, 1, 0) + jnp.where(me < nb - 1, 1, 0))

    def up_copy(n):
        return pltpu.make_async_remote_copy(
            src_ref=sbuf.at[n, 0], dst_ref=rlow.at[n],
            send_sem=send_sem.at[n, 0], recv_sem=recv_sem.at[n, 0],
            device_id={"brick": me + 1}, device_id_type=MESH,
        )

    def down_copy(n):
        return pltpu.make_async_remote_copy(
            src_ref=sbuf.at[n, 1], dst_ref=rhigh.at[n],
            send_sem=send_sem.at[n, 1], recv_sem=recv_sem.at[n, 1],
            device_id={"brick": me - 1}, device_id_type=MESH,
        )

    FR = E * E

    def send(n):
        for s in range(S):
            for i in range(E):
                base = at(s, i + 1, 1)
                high[pl.ds(s * FR + i * E, E), :] = pad[pl.ds(base + E, E, stride=R), :]
                low[pl.ds((S + s) * FR + i * E, E), :] = pad[pl.ds(base + 2 * E - 1, E, stride=R), :]
        m = left((FR, L))
        for q in range(S // 2):
            even, odd = 2 * q, 2 * q + 1
            sbuf[n, 0, pl.ds(q * FR, FR), :] = jnp.where(
                m, low[pl.ds((S + even) * FR, FR), :], low[pl.ds((S + odd) * FR, FR), :]
            ).astype(BF16)
            sbuf[n, 1, pl.ds(q * FR, FR), :] = jnp.where(
                m, high[pl.ds(even * FR, FR), :], high[pl.ds(odd * FR, FR), :]
            ).astype(BF16)

        @pl.when(me < nb - 1)
        def _():
            up_copy(n).start()

        @pl.when(me > 0)
        def _():
            down_copy(n).start()

    def matches(s, d, places):
        t = nbr_ref[s, d]
        t = jnp.where(t >= 0, t - me * S, -4 * S)
        return [t == k for k in places]

    def ring():
        def one(s, carry):
            for (a, b, c), d in number_of.items():
                if c != 0:
                    continue
                is_slot = matches(s, d, [k for k in range(S)])
                for i in range(E) if a == 0 else [E - 1 if a < 0 else 0]:
                    for j in range(E) if b == 0 else [E - 1 if b < 0 else 0]:
                        di = i + 1 if a == 0 else (0 if a < 0 else E + 1)
                        dj = j + 1 if b == 0 else (0 if b < 0 else E + 1)
                        v = jnp.zeros((E, L), F32)
                        for k in range(S):
                            v = jnp.where(is_slot[k], pad[pl.ds(at(k, i + 1, j + 1) + E, E), :], v)
                        dst = pl.multiple_of(at(s, di, dj) + E, E)
                        pad[pl.ds(dst, E), :] = v
            return carry

        lax.fori_loop(0, S, one, 0)

    def receive(n):
        m = left((FR, L))

        def unpack(ref, pool, first):
            for q in range(S // 2):
                v = ref[n, pl.ds(q * FR, FR), :].astype(F32)
                w = swap(v)
                pool[pl.ds((first + 2 * q) * FR, FR), :] = jnp.where(m, v, w)
                pool[pl.ds((first + 2 * q + 1) * FR, FR), :] = jnp.where(m, w, v)

        @pl.when(me > 0)
        def _():
            up_copy(n).wait_recv()
            unpack(rlow, low, 0)

        @pl.when(me < nb - 1)
        def _():
            down_copy(n).wait_recv()
            unpack(rhigh, high, S)

    def faces():
        def one(s, carry):
            for (a, b, c), d in number_of.items():
                if c == 0:
                    continue
                pool, row = (low, E - 1) if c < 0 else (high, 2 * E)
                is_slot = matches(s, d, [k - S if c < 0 else k for k in range(2 * S)])

                def pick(rows):
                    v = None
                    for k in range(2 * S):
                        u = pool[rows(k * FR), :]
                        v = jnp.where(is_slot[k], u, jnp.zeros_like(u) if v is None else v)
                    return v

                edge = lambda o: (E - 1, 0) if o < 0 else (0, E + 1)
                if b == 0:
                    for i in range(E) if a == 0 else [edge(a)[0]]:
                        di = i + 1 if a == 0 else edge(a)[1]
                        v = pick(lambda t: pl.ds(t + i * E, E))
                        pad[pl.ds(at(s, di, 1) + row, E, stride=R), :] = v
                elif a == 0:
                    j, dj = edge(b)
                    v = pick(lambda t: pl.ds(t + j, E, stride=E))
                    pad[pl.ds(at(s, 1, dj) + row, E, stride=R * G), :] = v
                else:
                    (i, di), (j, dj) = edge(a), edge(b)
                    v = pick(lambda t: pl.ds(t + i * E + j, 1))
                    pad[pl.ds(at(s, di, dj) + row, 1), :] = v
            return carry

        lax.fori_loop(0, S, one, 0)

    def build(x):
        def one(i, carry):
            m = left((E, L))
            for j in range(G):
                for s in range(0, S, 2):
                    a, b = [], []
                    for k in (s, s + 1):
                        base = pl.multiple_of(at(k, i, j), E)
                        here = pad[pl.ds(base + E, E), :]
                        a.append(jnp.where(m, pad[pl.ds(base + E - 1, E), :], here))
                        b.append(pad[pl.ds(base + E + 1, E), :])
                    r = j * jr + s * E
                    x[i, r : r + 2 * E, :L] = jnp.concatenate(a, axis=0).astype(BF16)
                    x[i, r : r + 2 * E, L:] = jnp.concatenate(b, axis=0).astype(BF16)
            return carry

        lax.fori_loop(0, G, one, 0)

    def put(i, v):
        for s in range(S):
            for j in range(E):
                pad[pl.ds(pl.multiple_of(at(s, i + 1, j + 1) + E, E), E), :] = v[
                    j * jr + s * E : j * jr + (s + 1) * E
                ]

    place = (0, 1, 2, 0)

    def forward_weights(w_ref, w):
        for a in range(3):
            for c in range(3):
                blocks = [w_ref[9 * a + 3 * b + c] for b in place]
                w[pl.ds(a * 4 * C + c * C, C), :] = jnp.concatenate(blocks, axis=1).astype(BF16)
            w[pl.ds(a * 4 * C + 3 * C, C), :] = jnp.zeros((C, 4 * C), BF16)

    def backward_weights(w_ref, w):
        for n, b in enumerate(place):
            for a in range(3):
                blocks = [w_ref[26 - (9 * a + 3 * b + c)] for c in range(3)]
                blocks.append(jnp.zeros((C, C), F32))
                w[pl.ds(n * C, C), pl.ds(a * 4 * C, 4 * C)] = jnp.concatenate(
                    blocks, axis=1
                ).astype(BF16)

    def conv(x, w, back, finish):
        def one(h, carry):
            parts = []
            for u in range(2):
                i = 2 * h + u
                parts.append(jnp.concatenate([x[i], x[i + 1], x[i + 2]], axis=1))
            y = lax.dot_general(
                jnp.concatenate(parts, axis=0), w[...],
                (((1,), (1 if back else 0,)), ((), ())), preferred_element_type=F32,
            )
            m = left((rows, L))
            done = []
            for u in range(2):
                p = y[u * G * jr : (u + 1) * G * jr, :L]
                q = y[u * G * jr : (u + 1) * G * jr, L:]
                p0, p1 = p[:rows], p[jr : jr + rows]
                q0, q2 = q[:rows], q[2 * jr : 2 * jr + rows]
                done.append(
                    jnp.where(m, p0, p1) + jnp.where(m, q2, q0) + swap(jnp.where(m, q2, p1))
                )
            finish(h, done)
            return carry

        lax.fori_loop(0, E // 2, one, 0)

    def put_errors(h, errs):
        parts = []
        z = jnp.zeros((jr, L), F32)
        m = left((G * jr, L))
        for e in errs:
            p0 = jnp.concatenate([e, z, z], axis=0)
            p1 = jnp.concatenate([z, e, z], axis=0)
            p2 = jnp.concatenate([z, z, e], axis=0)
            parts.append(jnp.concatenate([jnp.where(m, p0, p1), p2], axis=1).astype(BF16))
        t = jnp.concatenate(parts, axis=0).T
        et[h] = t

    def kernel_grad(x, g_out):
        for a in range(3):
            acc = jnp.zeros((3 * C, 4 * C), F32)
            for h in range(E // 2):
                xs = jnp.concatenate([x[2 * h + a], x[2 * h + a + 1]], axis=0)
                acc += jnp.dot(et[h, : 3 * C, :], xs, preferred_element_type=F32)
            g_out[a] = acc

    send(0)
    ring()
    forward_weights(w1_ref, w1f)
    forward_weights(w2_ref, w2f)
    receive(0)
    faces()
    build(x1)

    def first(h, ys):
        for u in range(2):
            i = 2 * h + u
            y = ys[u]
            fpre[i] = y
            hid = fin[i] + y * sigmoid(y)
            fhid[i] = hid
            put(i, hid)

    conv(x1, w1f, False, first)

    send(1)
    ring()
    backward_weights(w1_ref, w1b)
    backward_weights(w2_ref, w2b)
    receive(1)
    faces()
    build(x2)

    def second(h, ys):
        errs = []
        for u in range(2):
            i = 2 * h + u
            y = ys[u]
            q = sigmoid(y)
            fout[i] = fhid[i] + y * q
            err = fup[i] * (q * (1.0 + y * (1.0 - q)))
            put(i, err)
            errs.append(err)
        put_errors(h, errs)

    conv(x2, w2f, False, second)

    send(2)
    ring()
    kernel_grad(x2, g2_ref)
    receive(2)
    faces()
    build(x3)

    def third(h, ys):
        errs = []
        for u in range(2):
            i = 2 * h + u
            grad = fup[i] + ys[u]
            fhid[i] = grad
            y = fpre[i]
            q = sigmoid(y)
            err = grad * (q * (1.0 + y * (1.0 - q)))
            put(i, err)
            errs.append(err)
        put_errors(h, errs)

    conv(x3, w2b, True, third)

    send(3)
    ring()
    kernel_grad(x1, g1_ref)
    receive(3)
    faces()
    build(x2)

    def fourth(h, ys):
        both = []
        for u in range(2):
            i = 2 * h + u
            both.append(jnp.where(left((rows, L)), fout[i], fhid[i] + ys[u]))
        for s in range(S):
            v = jnp.concatenate(
                [
                    both[u][j * jr + s * E : j * jr + (s + 1) * E]
                    for u in range(2)
                    for j in range(E)
                ],
                axis=0,
            ).T
            cols = pl.ds(pl.multiple_of(h * 2 * E * E, 2 * E * E), 2 * E * E)
            out_ref[0, s, :, cols] = v[:C]
            fg_ref[0, s, :, cols] = v[C:]

    conv(x2, w1b, True, fourth)

    @pl.when(me < nb - 1)
    def _():
        for n in range(4):
            up_copy(n).wait_send()

    @pl.when(me > 0)
    def _():
        for n in range(4):
            down_copy(n).wait_send()


def body(features, cotangent, first_kernel, second_kernel, counts, neighbours):
    scenes_here, S, C, V = features.shape
    nb = lax.axis_size("brick")
    jr = S * E
    rows = E * jr
    vmem = pl.BlockSpec(memory_space=pltpu.VMEM)
    smem = pl.BlockSpec(memory_space=pltpu.SMEM)
    field = pltpu.VMEM((E, rows, L), F32)
    windows = pltpu.VMEM((G, G * jr, 2 * L), BF16)
    out, fg, g1, g2 = pl.pallas_call(
        functools.partial(kernel, nb, S),
        out_shape=[
            jax.ShapeDtypeStruct(features.shape, F32),
            jax.ShapeDtypeStruct(features.shape, F32),
            jax.ShapeDtypeStruct((3, 3 * C, 4 * C), F32),
            jax.ShapeDtypeStruct((3, 3 * C, 4 * C), F32),
        ],
        in_specs=[vmem] * 4 + [smem] * 2,
        out_specs=[vmem] * 4,
        scratch_shapes=[
            pltpu.VMEM((S * G * G * R, L), F32),
            windows, windows, windows,
            pltpu.VMEM((12 * C, 4 * C), BF16),
            pltpu.VMEM((12 * C, 4 * C), BF16),
            pltpu.VMEM((4 * C, 12 * C), BF16),
            pltpu.VMEM((4 * C, 12 * C), BF16),
            pltpu.VMEM((E // 2, 4 * C, 2 * G * jr), BF16),
            field, field, field, field, field,
            pltpu.VMEM((2 * S * E * E, L), F32),
            pltpu.VMEM((2 * S * E * E, L), F32),
            pltpu.VMEM((4, 2, S // 2 * E * E, L), BF16),
            pltpu.VMEM((4, S // 2 * E * E, L), BF16),
            pltpu.VMEM((4, S // 2 * E * E, L), BF16),
            pltpu.SemaphoreType.DMA((4, 2)),
            pltpu.SemaphoreType.DMA((4, 2)),
        ],
        compiler_params=pltpu.CompilerParams(
            collective_id=0, has_side_effects=True, vmem_limit_bytes=52 * 2**20
        ),
    )(features, cotangent, first_kernel, second_kernel, counts, neighbours)
    g1, g2 = lax.psum((g1[..., : 3 * C], g2[..., : 3 * C]), ("brick", "scene"))
    total = nb * lax.axis_size("scene") * scenes_here * S * V
    scale = 1.0 / jnp.sqrt(jnp.float32(total))

    def whole(g):
        g = g.reshape(3, 3, C, 3, C)
        return jnp.transpose(g, (0, 1, 3, 4, 2)).reshape(27, C, C) * scale

    return out, fg, whole(g1), whole(g2)


def solution(mesh):
    return jax.shard_map(
        body,
        mesh=mesh,
        in_specs=(
            P("scene", "brick", None, None),
            P("scene", "brick", None, None),
            P(),
            P(),
            P("brick"),
            P("brick", None),
        ),
        out_specs=(P("scene", "brick", None, None), P("scene", "brick", None, None), P(), P()),
        check_vma=False,
    )
```

profile of v0, /device:TPU:1, one launch (start us, length us, event | category | flops | bytes accessed | tf_op | source)
XLA Modules:
  0.0 186.5 jit_solution(16640555450485624308)
XLA Ops:
  7.2 0.0 all-reduce.3.cloned.1.call-start
  7.9 0.0 copy-start
  7.9 1.0 copy-done
  8.9 0.0 copy-start.1
  8.9 0.7 copy-done.1
  9.6 29.1 %shard_map.93 = (f32[1,4,64,512]{3,2,1,0:T(8,128)S(1)}, f32[1,4,64,512]{3,2,1,0:T(8,128)S(1)}, f32[3,192,256]{2,1,0:T(8,128)}, f32[3,192,256]{2,1,0:T(8,128)}) custom-call(f32[1,4,64,512]{3,2,1,0:T(8,128)S(1)} %copy-done, f32[1,4,64,512]{3,2,1,0:T(8,128)} %g_ref.1, f32[27,64,64]{2,1,0:T(8,128)} %w1_ref.1, f32[27,64,64]{2,1,0:T(8,128)} %w2_ref.1, ...), custom_call_target="tpu_custom_call" | custom-call | tf_op jit(solution)/shard_map/pallas_call | solution.py:395
  38.7 0.0 all-reduce.3.cloned.1.call-update
  38.8 134.3 %all-reduce.3.cloned.1.call-done = (f32[3,192,192]{2,1,0:T(8,128)}, f32[3,192,192]{2,1,0:T(8,128)}) async-done(((f32[3,192,192]{2,1,0:T(8,128)}, f32[3,192,192]{2,1,0:T(8,128)}), (f32[3,192,192]{2,1,0:T(8,128)}, f32[3,192,192]{2,1,0:T(8,128)})) %all-reduce.3.cloned.1.call-update) | async-done | bytes 884752 | tf_op jit(solution)/shard_map/psum | solution.py:426
  173.1 1.3 broadcast_multiply_fusion
  174.4 0.4 mul.29
  174.8 1.5 copy.13
  176.3 0.4 mul.25
  176.6 1.5 copy.12
  178.1 0.8 copy.19
  178.9 0.8 copy.20
Async XLA Ops:
  7.2 165.9 %all-reduce.3.cloned.1.call-start = ((), (), s32[]{:S(2)}) async-start(), calls=%async_computation | async-start | bytes 2359296 | tf_op jit(solution)/shard_map/psum | solution.py:426
  7.9 1.0 copy-start
  8.9 0.7 copy-start.1
Sparse Core Ops, SparseCore 0:
  38.9 134.1 all-reduce.2
where the time goes:
time: 188 us; the launch traced here: 187 us
  waiting for transfers between devices  134 us (71%)
  Pallas kernels  29.1 us (15%)
  between operations  14.7 us (8%)
  local copies, waits for them, and re-layouts  6.92 us (4%)
    psum x1, waiting for transfers between devices, body(): g1, g2 = lax.psum((g1[..., :3 * C], g2[..., :3 * C]), ('brick', 'scene'))  134 us
    pallas_call x1, Pallas kernels, body(): pl.pallas_call(functools.partial(kernel, nb, S), out_shape=[jax.ShapeDtyp...  29.1 us
  transfers between devices with their start and end apart: 1, of which 1 were waited for; matrix products, arithmetic and copies ran while one was open for 0% of the time, Pallas kernels for 0%

commit v1 on v0

--- a/solution.py
+++ b/solution.py
@@ -32,12 +32,13 @@
 
 
 def kernel(
-    nb, S,
+    nb, ns, S, scale,
     f_ref, g_ref, w1_ref, w2_ref, counts_ref, nbr_ref,
     out_ref, fg_ref, g1_ref, g2_ref,
     pad, x1, x2, x3, w1f, w2f, w1b, w2b, et,
     fin, fup, fpre, fhid, fout, low, high, sbuf, rlow, rhigh,
-    send_sem, recv_sem,
+    part, from_scene, mine, from_brick, full,
+    send_sem, recv_sem, sum_send, sum_recv,
 ):
     C = w1_ref.shape[1]
     me = lax.axis_index("brick")
@@ -46,13 +47,11 @@
 
     barrier = pltpu.get_barrier_semaphore()
 
-    @pl.when(me > 0)
-    def _():
-        pl.semaphore_signal(barrier, inc=1, device_id={"brick": me - 1}, device_id_type=MESH)
-
-    @pl.when(me < nb - 1)
-    def _():
-        pl.semaphore_signal(barrier, inc=1, device_id={"brick": me + 1}, device_id_type=MESH)
+    sc = lax.axis_index("scene")
+    partners = [{"scene": lax.rem(sc + o, ns)} for o in range(1, ns)]
+    partners += [{"brick": lax.rem(me + o, nb)} for o in range(1, nb)]
+    for partner in partners:
+        pl.semaphore_signal(barrier, inc=1, device_id=partner, device_id_type=MESH)
 
     def at(s, i, j):
         return ((s * G + i) * G + j) * R
@@ -75,7 +74,7 @@
     low[...] = jnp.zeros_like(low)
     high[...] = jnp.zeros_like(high)
 
-    pl.semaphore_wait(barrier, jnp.where(me > 0, 1, 0) + jnp.where(me < nb - 1, 1, 0))
+    pl.semaphore_wait(barrier, len(partners))
 
     def up_copy(n):
         return pltpu.make_async_remote_copy(
@@ -274,13 +273,91 @@
         t = jnp.concatenate(parts, axis=0).T
         et[h] = t
 
-    def kernel_grad(x, g_out):
+    CR = 3 * C
+    total_rows = full.shape[1]
+    Q = total_rows // ns
+    q = Q // nb
+
+    def kernel_grad(x, n):
+        m = left((CR, L))
+        last = []
         for a in range(3):
-            acc = jnp.zeros((3 * C, 4 * C), F32)
+            acc = jnp.zeros((4 * C, 4 * C), F32)
             for h in range(E // 2):
                 xs = jnp.concatenate([x[2 * h + a], x[2 * h + a + 1]], axis=0)
-                acc += jnp.dot(et[h, : 3 * C, :], xs, preferred_element_type=F32)
-            g_out[a] = acc
+                acc += jnp.dot(et[h], xs, preferred_element_type=F32)
+            g = acc.T[:CR]
+            part[n, pl.ds(a * CR, CR), :] = g[:, :L].astype(BF16)
+            last.append(g[:, L:])
+        part[n, pl.ds(3 * CR, CR), :] = jnp.where(m, last[0], last[1]).astype(BF16)
+        part[n, pl.ds(4 * CR, CR), :] = last[2].astype(BF16)
+        rest = total_rows - 5 * CR
+        if rest:
+            part[n, pl.ds(5 * CR, rest), :] = jnp.zeros((rest, L), BF16)
+
+    def sum_copies(n, step):
+        copies = []
+        axis, size, here = ("scene", ns, sc) if step in (0, 3) else ("brick", nb, me)
+        first_sem = (0, ns - 1, ns + nb - 2, ns + 2 * nb - 3)[step]
+        for o in range(1, size):
+            to = lax.rem(here + o, size)
+            if step == 0:
+                src, dst = part.at[n, pl.ds(pl.multiple_of(to * Q, 16), Q)], from_scene.at[n, o - 1]
+            elif step == 1:
+                src, dst = mine.at[n, pl.ds(pl.multiple_of(to * q, 16), q)], from_brick.at[n, o - 1]
+            elif step == 2:
+                src = full.at[n, pl.ds(pl.multiple_of(sc * Q + me * q, 16), q)]
+                dst = src
+            else:
+                src = full.at[n, pl.ds(pl.multiple_of(sc * Q, 16), Q)]
+                dst = src
+            copies.append(
+                pltpu.make_async_remote_copy(
+                    src_ref=src, dst_ref=dst,
+                    send_sem=sum_send.at[n, first_sem + o - 1],
+                    recv_sem=sum_recv.at[n, first_sem + o - 1],
+                    device_id={axis: to}, device_id_type=MESH,
+                )
+            )
+        return copies
+
+    def sum_start(n, step):
+        for copy in sum_copies(n, step):
+            copy.start()
+
+    def sum_wait(n, step):
+        for copy in sum_copies(n, step):
+            copy.wait_recv()
+
+    def sum_next(n, step):
+        sum_wait(n, step)
+        if step == 0:
+            acc = part[n, pl.ds(pl.multiple_of(sc * Q, 16), Q), :].astype(F32)
+            for o in range(ns - 1):
+                acc += from_scene[n, o].astype(F32)
+            mine[n] = acc.astype(BF16)
+        elif step == 1:
+            acc = mine[n, pl.ds(pl.multiple_of(me * q, 16), q), :].astype(F32)
+            for o in range(nb - 1):
+                acc += from_brick[n, o].astype(F32)
+            full[n, pl.ds(pl.multiple_of(sc * Q + me * q, 16), q), :] = (acc * scale).astype(BF16)
+        sum_start(n, step + 1)
+
+    def sum_end(n, ref):
+        sum_wait(n, 3)
+
+        def put_blocks(a, b, v):
+            for c in range(3):
+                ref[9 * a + 3 * b + c] = v[c * C : (c + 1) * C, :C]
+
+        for a in range(3):
+            v = full[n, pl.ds(a * CR, CR), :].astype(F32)
+            put_blocks(a, 0, v)
+            put_blocks(a, 1, swap(v))
+        v = full[n, pl.ds(3 * CR, CR), :].astype(F32)
+        put_blocks(0, 2, v)
+        put_blocks(1, 2, swap(v))
+        put_blocks(2, 2, full[n, pl.ds(4 * CR, CR), :].astype(F32))
 
     send(0)
     ring()
@@ -325,7 +402,8 @@
 
     send(2)
     ring()
-    kernel_grad(x2, g2_ref)
+    kernel_grad(x2, 1)
+    sum_start(1, 0)
     receive(2)
     faces()
     build(x3)
@@ -347,8 +425,11 @@
 
     send(3)
     ring()
-    kernel_grad(x1, g1_ref)
+    sum_next(1, 0)
+    kernel_grad(x1, 0)
+    sum_start(0, 0)
     receive(3)
+    sum_next(1, 1)
     faces()
     build(x2)
 
@@ -370,7 +451,18 @@
             out_ref[0, s, :, cols] = v[:C]
             fg_ref[0, s, :, cols] = v[C:]
 
+    sum_next(0, 0)
+    sum_next(1, 2)
     conv(x2, w1b, True, fourth)
+
+    sum_next(0, 1)
+    sum_end(1, g2_ref)
+    sum_next(0, 2)
+    sum_end(0, g1_ref)
+    for n in range(2):
+        for step in range(4):
+            for copy in sum_copies(n, step):
+                copy.wait_send()
 
     @pl.when(me < nb - 1)
     def _():
@@ -385,7 +477,10 @@
 
 def body(features, cotangent, first_kernel, second_kernel, counts, neighbours):
     scenes_here, S, C, V = features.shape
-    nb = lax.axis_size("brick")
+    nb, ns = lax.axis_size("brick"), lax.axis_size("scene")
+    total = nb * ns * scenes_here * S * V
+    blocks = 16 * nb * ns
+    total_rows = -(-15 * C // blocks) * blocks
     jr = S * E
     rows = E * jr
     vmem = pl.BlockSpec(memory_space=pltpu.VMEM)
@@ -393,12 +488,12 @@
     field = pltpu.VMEM((E, rows, L), F32)
     windows = pltpu.VMEM((G, G * jr, 2 * L), BF16)
     out, fg, g1, g2 = pl.pallas_call(
-        functools.partial(kernel, nb, S),
+        functools.partial(kernel, nb, ns, S, float(total) ** -0.5),
         out_shape=[
             jax.ShapeDtypeStruct(features.shape, F32),
             jax.ShapeDtypeStruct(features.shape, F32),
-            jax.ShapeDtypeStruct((3, 3 * C, 4 * C), F32),
-            jax.ShapeDtypeStruct((3, 3 * C, 4 * C), F32),
+            jax.ShapeDtypeStruct(first_kernel.shape, F32),
+            jax.ShapeDtypeStruct(first_kernel.shape, F32),
         ],
         in_specs=[vmem] * 4 + [smem] * 2,
         out_specs=[vmem] * 4,
@@ -416,22 +511,21 @@
             pltpu.VMEM((4, 2, S // 2 * E * E, L), BF16),
             pltpu.VMEM((4, S // 2 * E * E, L), BF16),
             pltpu.VMEM((4, S // 2 * E * E, L), BF16),
+            pltpu.VMEM((2, total_rows, L), BF16),
+            pltpu.VMEM((2, ns - 1, total_rows // ns, L), BF16),
+            pltpu.VMEM((2, total_rows // ns, L), BF16),
+            pltpu.VMEM((2, nb - 1, total_rows // ns // nb, L), BF16),
+            pltpu.VMEM((2, total_rows, L), BF16),
             pltpu.SemaphoreType.DMA((4, 2)),
             pltpu.SemaphoreType.DMA((4, 2)),
+            pltpu.SemaphoreType.DMA((2, 2 * (nb + ns - 2))),
+            pltpu.SemaphoreType.DMA((2, 2 * (nb + ns - 2))),
         ],
         compiler_params=pltpu.CompilerParams(
             collective_id=0, has_side_effects=True, vmem_limit_bytes=52 * 2**20
         ),
     )(features, cotangent, first_kernel, second_kernel, counts, neighbours)
-    g1, g2 = lax.psum((g1[..., : 3 * C], g2[..., : 3 * C]), ("brick", "scene"))
-    total = nb * lax.axis_size("scene") * scenes_here * S * V
-    scale = 1.0 / jnp.sqrt(jnp.float32(total))
-
-    def whole(g):
-        g = g.reshape(3, 3, C, 3, C)
-        return jnp.transpose(g, (0, 1, 3, 4, 2)).reshape(27, C, C) * scale
-
-    return out, fg, whole(g1), whole(g2)
+    return out, fg, g1, g2
 
 
 def solution(mesh):

time: 188 us -> 56.9 us (0.30)
  waiting for transfers between devices: 134 us -> 0 us
  Pallas kernels: 29.1 us -> 49.6 us
  between operations: 14.7 us -> 1.31 us
    psum x1 -> x0, waiting for transfers between devices: 134 us -> none  [body(): g1, g2 = lax.psum((g1[..., :3 * C], g2[..., :3 * C]), ('brick', 'scene'))]
    pallas_call x1, Pallas kernels: 29.1 us -> 49.6 us  [body(): pl.pallas_call(functools.partial(kernel, nb, ns, S, float(total) ** (-0.5...]
    mul x4 -> x0, local copies, waits for them, and re-layouts: 3.62 us -> none  [whole(): return jnp.transpose(g, (0, 1, 3, 4, 2)).reshape(27, C, C) * scale]
    unnamed x6 -> x12, local copies, waits for them, and re-layouts: 3.3 us -> 5.71 us
  transfers between devices with their start and end apart: 1 -> 0, of which waited for: 1 -> 0; matrix products, arithmetic and copies ran while one was open for 0% -> 0% of each run, Pallas kernels for 0% -> 0%
where the time goes in v1:
time: 56.9 us; the launch traced here: 56.6 us
  Pallas kernels  49.6 us (87%)
  local copies, waits for them, and re-layouts  5.71 us (10%)
  between operations  1.31 us (2%)
    pallas_call x1, Pallas kernels, body(): pl.pallas_call(functools.partial(kernel, nb, ns, S, float(total) ** (-0.5...  49.6 us
    unnamed x12, local copies, waits for them, and re-layouts  5.71 us

profile of v1, /device:TPU:1, one launch (start us, length us, event | category | flops | bytes accessed | tf_op | source)
XLA Modules:
  0.0 56.6 jit_solution(18333846736311479260)
XLA Ops:
  1.3 0.0 copy-start
  1.3 1.0 %copy-done = f32[1,4,64,512]{3,2,1,0:T(8,128)S(1)} copy-done((f32[1,4,64,512]{3,2,1,0:T(8,128)S(1)}, f32[1,4,64,512]{3,2,1,0:T(8,128)}, u32[]{:S(2)}) %copy-start) | copy-done | bytes 524312
  2.3 0.0 copy-start.1
  2.3 0.7 %copy-done.1 = s32[4,26]{1,0:T(4,128)S(1)} copy-done((s32[4,26]{1,0:T(4,128)S(1)}, s32[4,26]{1,0:T(4,128)}, u32[]{:S(2)}) %copy-start.1) | copy-done | bytes 440
  3.0 49.6 %shard_map.93 = (f32[1,4,64,512]{3,2,1,0:T(8,128)S(1)}, f32[1,4,64,512]{3,2,1,0:T(8,128)S(1)}, f32[27,64,64]{2,1,0:T(8,128)}, f32[27,64,64]{2,1,0:T(8,128)}) custom-call(f32[1,4,64,512]{3,2,1,0:T(8,128)S(1)} %copy-done, f32[1,4,64,512]{3,2,1,0:T(8,128)} %g_ref.1, f32[27,64,64]{2,1,0:T(8,128)} %w1_ref.1, f32[27,64,64]{2,1,0:T(8,128)} %w2_ref.1, ...), custom_call_target="tpu_custom_call" | custom-call | tf_op jit(solution)/shard_map/pallas_call | solution.py:490
  52.6 0.0 copy-start.3
  52.6 0.8 %copy.15 = f32[1,4,64,512]{3,2,1,0:T(8,128)} copy(f32[1,4,64,512]{3,2,1,0:T(8,128)S(1)} %get-tuple-element.8) | data formatting | bytes 1048576
  53.4 0.8 %copy.16 = f32[1,4,64,512]{3,2,1,0:T(8,128)} copy(f32[1,4,64,512]{3,2,1,0:T(8,128)S(1)} %get-tuple-element.9) | data formatting | bytes 1048576
  54.2 0.0 copy-done.3
  54.2 0.0 copy-start.2
  54.2 0.9 %copy.17 = f32[27,64,64]{2,1,0:T(8,128)} copy(f32[27,64,64]{2,1,0:T(8,128)S(1)} %copy-done.3) | data formatting | bytes 884736
  55.1 0.6 %copy-done.2 = f32[27,64,64]{2,1,0:T(8,128)S(1)} copy-done((f32[27,64,64]{2,1,0:T(8,128)S(1)}, f32[27,64,64]{2,1,0:T(8,128)}, u32[]{:S(2)}) %copy-start.2) | copy-done | bytes 442392
  55.7 0.9 %copy.18 = f32[27,64,64]{2,1,0:T(8,128)} copy(f32[27,64,64]{2,1,0:T(8,128)S(1)} %copy-done.2) | data formatting | bytes 884736
Async XLA Ops:
  1.3 1.0 %copy-start = (f32[1,4,64,512]{3,2,1,0:T(8,128)S(1)}, f32[1,4,64,512]{3,2,1,0:T(8,128)}, u32[]{:S(2)}) copy-start(f32[1,4,64,512]{3,2,1,0:T(8,128)} %f_ref.1) | copy-start | bytes 1572868
  2.3 0.7 %copy-start.1 = (s32[4,26]{1,0:T(4,128)S(1)}, s32[4,26]{1,0:T(4,128)}, u32[]{:S(2)}) copy-start(s32[4,26]{1,0:T(4,128)} %nbr_ref.1) | copy-start | bytes 1252
  52.6 1.6 %copy-start.3 = (f32[27,64,64]{2,1,0:T(8,128)S(1)}, f32[27,64,64]{2,1,0:T(8,128)}, u32[]{:S(2)}) copy-start(f32[27,64,64]{2,1,0:T(8,128)} %get-tuple-element.10) | copy-start | bytes 1327108
  54.2 1.5 %copy-start.2 = (f32[27,64,64]{2,1,0:T(8,128)S(1)}, f32[27,64,64]{2,1,0:T(8,128)}, u32[]{:S(2)}) copy-start(f32[27,64,64]{2,1,0:T(8,128)} %get-tuple-element.11) | copy-start | bytes 1327108

commit v2 on v1

--- a/solution.py
+++ b/solution.py
@@ -236,7 +236,7 @@
                     blocks, axis=1
                 ).astype(BF16)
 
-    def conv(x, w, back, finish):
+    def conv(x, w, back, finish, first=0, end=E // 2):
         def one(h, carry):
             parts = []
             for u in range(2):
@@ -259,7 +259,7 @@
             finish(h, done)
             return carry
 
-        lax.fori_loop(0, E // 2, one, 0)
+        lax.fori_loop(first, end, one, 0)
 
     def put_errors(h, errs):
         parts = []
@@ -271,7 +271,7 @@
             p2 = jnp.concatenate([z, z, e], axis=0)
             parts.append(jnp.concatenate([jnp.where(m, p0, p1), p2], axis=1).astype(BF16))
         t = jnp.concatenate(parts, axis=0).T
-        et[h] = t
+        et[:, pl.ds(pl.multiple_of(h * 2 * G * jr, L), 2 * G * jr)] = t
 
     CR = 3 * C
     total_rows = full.shape[1]
@@ -282,10 +282,8 @@
         m = left((CR, L))
         last = []
         for a in range(3):
-            acc = jnp.zeros((4 * C, 4 * C), F32)
-            for h in range(E // 2):
-                xs = jnp.concatenate([x[2 * h + a], x[2 * h + a + 1]], axis=0)
-                acc += jnp.dot(et[h], xs, preferred_element_type=F32)
+            xs = x[a : a + E].reshape(E * G * jr, 4 * C)
+            acc = jnp.dot(et[...], xs, preferred_element_type=F32)
             g = acc.T[:CR]
             part[n, pl.ds(a * CR, CR), :] = g[:, :L].astype(BF16)
             last.append(g[:, L:])
@@ -401,9 +399,9 @@
     conv(x2, w2f, False, second)
 
     send(2)
-    ring()
     kernel_grad(x2, 1)
     sum_start(1, 0)
+    ring()
     receive(2)
     faces()
     build(x3)
@@ -424,14 +422,16 @@
     conv(x3, w2b, True, third)
 
     send(3)
-    ring()
     sum_next(1, 0)
     kernel_grad(x1, 0)
     sum_start(0, 0)
+    ring()
+    sum_next(1, 1)
     receive(3)
-    sum_next(1, 1)
     faces()
     build(x2)
+    sum_next(0, 0)
+    sum_next(1, 2)
 
     def fourth(h, ys):
         both = []
@@ -451,13 +451,12 @@
             out_ref[0, s, :, cols] = v[:C]
             fg_ref[0, s, :, cols] = v[C:]
 
-    sum_next(0, 0)
-    sum_next(1, 2)
-    conv(x2, w1b, True, fourth)
-
+    conv(x2, w1b, True, fourth, 0, E // 4)
     sum_next(0, 1)
+    conv(x2, w1b, True, fourth, E // 4, E // 2)
+
+    sum_next(0, 2)
     sum_end(1, g2_ref)
-    sum_next(0, 2)
     sum_end(0, g1_ref)
     for n in range(2):
         for step in range(4):
@@ -504,7 +503,7 @@
             pltpu.VMEM((12 * C, 4 * C), BF16),
             pltpu.VMEM((4 * C, 12 * C), BF16),
             pltpu.VMEM((4 * C, 12 * C), BF16),
-            pltpu.VMEM((E // 2, 4 * C, 2 * G * jr), BF16),
+            pltpu.VMEM((4 * C, E * G * jr), BF16),
             field, field, field, field, field,
             pltpu.VMEM((2 * S * E * E, L), F32),
             pltpu.VMEM((2 * S * E * E, L), F32),

time: 56.9 us -> 55.3 us (0.972)
  Pallas kernels: 49.6 us -> 48.1 us
    pallas_call x1, Pallas kernels: 49.6 us -> 48.1 us  [body(): pl.pallas_call(functools.partial(kernel, nb, ns, S, float(total) ** (-0.5...]
where the time goes in v2:
time: 55.3 us; the launch traced here: 55.1 us
  Pallas kernels  48.1 us (87%)
  local copies, waits for them, and re-layouts  5.71 us (10%)
  between operations  1.31 us (2%)
    pallas_call x1, Pallas kernels, body(): pl.pallas_call(functools.partial(kernel, nb, ns, S, float(total) ** (-0.5...  48.1 us
    unnamed x12, local copies, waits for them, and re-layouts  5.71 us

profile of v2, /device:TPU:1, one launch (start us, length us, event | category | flops | bytes accessed | tf_op | source)
XLA Modules:
  0.0 55.1 jit_solution(17874334304721509231)
XLA Ops:
  1.3 0.0 copy-start
  1.3 1.0 %copy-done = f32[1,4,64,512]{3,2,1,0:T(8,128)S(1)} copy-done((f32[1,4,64,512]{3,2,1,0:T(8,128)S(1)}, f32[1,4,64,512]{3,2,1,0:T(8,128)}, u32[]{:S(2)}) %copy-start) | copy-done | bytes 524312
  2.3 0.0 copy-start.1
  2.3 0.7 %copy-done.1 = s32[4,26]{1,0:T(4,128)S(1)} copy-done((s32[4,26]{1,0:T(4,128)S(1)}, s32[4,26]{1,0:T(4,128)}, u32[]{:S(2)}) %copy-start.1) | copy-done | bytes 440
  3.0 48.1 %shard_map.93 = (f32[1,4,64,512]{3,2,1,0:T(8,128)S(1)}, f32[1,4,64,512]{3,2,1,0:T(8,128)S(1)}, f32[27,64,64]{2,1,0:T(8,128)}, f32[27,64,64]{2,1,0:T(8,128)}) custom-call(f32[1,4,64,512]{3,2,1,0:T(8,128)S(1)} %copy-done, f32[1,4,64,512]{3,2,1,0:T(8,128)} %g_ref.1, f32[27,64,64]{2,1,0:T(8,128)} %w1_ref.1, f32[27,64,64]{2,1,0:T(8,128)} %w2_ref.1, ...), custom_call_target="tpu_custom_call" | custom-call | tf_op jit(solution)/shard_map/pallas_call | solution.py:489
  51.1 0.0 copy-start.3
  51.1 0.8 %copy.15 = f32[1,4,64,512]{3,2,1,0:T(8,128)} copy(f32[1,4,64,512]{3,2,1,0:T(8,128)S(1)} %get-tuple-element.8) | data formatting | bytes 1048576
  51.9 0.8 %copy.16 = f32[1,4,64,512]{3,2,1,0:T(8,128)} copy(f32[1,4,64,512]{3,2,1,0:T(8,128)S(1)} %get-tuple-element.9) | data formatting | bytes 1048576
  52.7 0.0 copy-done.3
  52.7 0.0 copy-start.2
  52.7 0.9 %copy.17 = f32[27,64,64]{2,1,0:T(8,128)} copy(f32[27,64,64]{2,1,0:T(8,128)S(1)} %copy-done.3) | data formatting | bytes 884736
  53.6 0.6 %copy-done.2 = f32[27,64,64]{2,1,0:T(8,128)S(1)} copy-done((f32[27,64,64]{2,1,0:T(8,128)S(1)}, f32[27,64,64]{2,1,0:T(8,128)}, u32[]{:S(2)}) %copy-start.2) | copy-done | bytes 442392
  54.2 0.9 %copy.18 = f32[27,64,64]{2,1,0:T(8,128)} copy(f32[27,64,64]{2,1,0:T(8,128)S(1)} %copy-done.2) | data formatting | bytes 884736
Async XLA Ops:
  1.3 1.0 %copy-start = (f32[1,4,64,512]{3,2,1,0:T(8,128)S(1)}, f32[1,4,64,512]{3,2,1,0:T(8,128)}, u32[]{:S(2)}) copy-start(f32[1,4,64,512]{3,2,1,0:T(8,128)} %f_ref.1) | copy-start | bytes 1572868
  2.3 0.7 %copy-start.1 = (s32[4,26]{1,0:T(4,128)S(1)}, s32[4,26]{1,0:T(4,128)}, u32[]{:S(2)}) copy-start(s32[4,26]{1,0:T(4,128)} %nbr_ref.1) | copy-start | bytes 1252
  51.1 1.6 %copy-start.3 = (f32[27,64,64]{2,1,0:T(8,128)S(1)}, f32[27,64,64]{2,1,0:T(8,128)}, u32[]{:S(2)}) copy-start(f32[27,64,64]{2,1,0:T(8,128)} %get-tuple-element.10) | copy-start | bytes 1327108
  52.7 1.5 %copy-start.2 = (f32[27,64,64]{2,1,0:T(8,128)S(1)}, f32[27,64,64]{2,1,0:T(8,128)}, u32[]{:S(2)}) copy-start(f32[27,64,64]{2,1,0:T(8,128)} %get-tuple-element.11) | copy-start | bytes 1327108
